TPU v7x, 32 devices: a whole 2x2x4 slice. The times are simulated.
32 devices in a mesh: blk: 16 (over z, y, x), grp: 2 (over core).
Axes of the slice: x: 2, y: 2, z: 4, core: 2. Of those that a mesh axis runs over, the one named last changes fastest.
Arguments:
- samples: float32 [32, 1024], P(None, ('blk', 'grp')), may hold values from 0 to 256
- bounds: int32 [2, 32, 2048], P(None, None, 'blk'), may hold values from 0 to 256, as said below
- spread: float32 [32], replicated, may hold values from 2 to 8
- counts: int32 [2048], P('blk'), may hold values from 0 to 2047
Outputs:
- log_estimate: float32 [2048], P('blk')
- spread_grad: float32 [32], replicated
Inputs may be any that keep to these rules, and one draw needn't show every extreme that they name: For every query and dimension bounds[0] < bounds[1]; each query restricts exactly 3 dimensions to a width of 16 to 48 cells and has bounds 0 and 256 in all others.
All inputs are finite; a program needn't handle non-finite values.
Results may differ from a plain program's by a relative error of at most 0.0003.
Values sent between devices are 32-bit elements; how exact they have to be, the bound alone decides.
No kernel may reach another device: no remote copies, remote signals or barrier semaphores. Data moves between devices by JAX's collectives and lax.ppermute only.
A program may use at most 64 MiB of HBM per device.

v0:
```python
import functools

import jax
import jax.numpy as jnp
from jax import lax
from jax.experimental import pallas as pl
from jax.experimental.pallas import tpu as pltpu
from jax.sharding import PartitionSpec as P

TABLE_ROWS = 1048576
GRID = 256
LIMITED = 3

UNIT = 0.8493218002880191
SLOPE = 0.46971863934982566
ERF_UNIT = 0.8325546111576977


def end_terms(v):
    bell = jnp.exp2(-(v * v))
    return 0.5 * lax.erf(v * ERF_UNIT), v * bell


def box_terms(low, high):
    low_erf, low_bell = end_terms(low)
    high_erf, high_bell = end_terms(high)
    return high_erf - low_erf, SLOPE * (low_bell - high_bell)


def split(x, parts):
    out = []
    for _ in range(parts - 1):
        head = x.astype(jnp.bfloat16)
        out.append(head)
        x = x - head.astype(jnp.float32)
    return out + [x.astype(jnp.bfloat16)]


def tree_sum(parts):
    while len(parts) > 1:
        parts = [a + b for a, b in zip(parts[::2], parts[1::2])]
    return parts[0]


def pack_kernel(x_ref, bounds_ref, spread_ref, counts_ref, out_ref, target_ref):
    rows, width = x_ref.shape
    packed = jnp.concatenate([x_ref[8 * j : 8 * (j + 1), :] for j in range(rows // 8)], axis=1)
    for peer in range(out_ref.shape[0]):
        out_ref[peer] = packed
    smoothing = 1.0 / TABLE_ROWS
    target_ref[...] = jnp.log(counts_ref[...].astype(jnp.float32) / TABLE_ROWS + smoothing)


def terms_kernel(width, blocks_ref, bounds_ref, spread_ref, out_ref, picked, inside):
    dims, queries = bounds_ref.shape[1:]
    total = blocks_ref.shape[0] * width

    low, high = bounds_ref[0], bounds_ref[1]
    limited = (high - low) != GRID
    low, high = low.astype(jnp.float32), high.astype(jnp.float32)
    at = lax.broadcasted_iota(jnp.int32, (dims, queries), 0)
    first = jnp.min(jnp.where(limited, at, dims), axis=0, keepdims=True)
    last = jnp.max(jnp.where(limited, at, -1), axis=0, keepdims=True)
    is_first, is_last = at == first, at == last
    chosen = [is_first, limited & (at > first) & (at < last), is_last]

    row = lax.broadcasted_iota(jnp.int32, (dims, dims), 0)
    column = lax.broadcasted_iota(jnp.int32, (dims, dims), 1)
    spread = jnp.sum(jnp.where(row == column, spread_ref[...], 0.0), axis=1, keepdims=True)
    unit = UNIT / spread

    pick = lambda mask, values: jnp.sum(jnp.where(mask, values, 0.0), axis=0, keepdims=True)
    low_at = [pick(mask, low) for mask in chosen]
    high_at = [pick(mask, high) for mask in chosen]
    unit_at = [pick(mask, unit) for mask in chosen]

    x = jnp.concatenate(
        [
            jnp.concatenate(
                [blocks_ref[b, :, width * j : width * (j + 1)] for b in range(blocks_ref.shape[0])],
                axis=1,
            )
            for j in range(dims // 8)
        ],
        axis=0,
    )
    full, full_slope = box_terms(-x * unit, (float(GRID) - x) * unit)
    ratio = full_slope / full
    left = jnp.concatenate(split(x, 3) + split(jnp.log(full), 3), axis=0)

    ones = [mask.astype(jnp.float32).astype(jnp.bfloat16) for mask in chosen]
    free = jnp.where(limited, 0.0, 1.0).astype(jnp.bfloat16)
    none = jnp.zeros_like(free)
    right = jnp.concatenate(
        [jnp.concatenate(ones + [none], axis=1)] * 3
        + [jnp.concatenate([none] * LIMITED + [free], axis=1)] * 3,
        axis=0,
    )
    picked[...] = lax.dot_general(
        left, right, (((0,), (0,)), ((), ())), preferred_element_type=jnp.float32
    )

    def advance(step, sums):
        rows = pl.ds(pl.multiple_of(step * 16, 16), 16)
        others = jnp.exp(picked[rows, LIMITED * queries :])
        mass, slope = [], []
        for k in range(LIMITED):
            points = picked[rows, k * queries : (k + 1) * queries]
            m, s = box_terms((low_at[k] - points) * unit_at[k], (high_at[k] - points) * unit_at[k])
            mass.append(m)
            slope.append(s)
        pair = others * mass[0]
        last_two = pair * mass[1]
        whole = last_two * mass[2]
        head, tail = split(whole, 2)
        inside[rows, :queries] = head
        inside[rows, queries:] = tail
        return (
            sums[0] + whole,
            sums[1] + others * mass[1] * mass[2] * slope[0],
            sums[2] + pair * mass[2] * slope[1],
            sums[3] + last_two * slope[2],
        )

    zero = jnp.zeros((16, queries), jnp.float32)
    sums = lax.fori_loop(0, total // 16, advance, (zero,) * 4, unroll=2)
    sums = [jnp.sum(s, axis=0, keepdims=True) for s in sums]

    ratio = jnp.concatenate(split(ratio, 2), axis=0)
    products = jnp.dot(ratio, inside[...], preferred_element_type=jnp.float32)
    deriv = products[:dims, :queries] + (products[dims:, :queries] + products[:dims, queries:])
    deriv = jnp.where(limited, 0.0, deriv)
    for mask, s in zip(chosen, sums[1:]):
        deriv = jnp.where(mask, s, deriv)
    out_ref[:dims, :] = deriv
    out_ref[dims:, :] = jnp.broadcast_to(sums[0], (8, queries))


def finish_kernel(sample_total, query_total, *refs):
    part_refs, (target_ref, log_ref, share_ref) = refs[:-3], refs[-3:]
    whole = tree_sum([ref[...] for ref in part_refs])
    dims, queries = whole.shape[0] - 8, whole.shape[1]
    smoothing = 1.0 / TABLE_ROWS
    estimate = whole[dims : dims + 1] / sample_total
    log_est = jnp.log(estimate + smoothing)
    log_ref[...] = log_est
    weight = 2.0 * (log_est - target_ref[...]) / (query_total * (estimate + smoothing))
    terms = whole[:dims] * (weight / sample_total)
    terms = jnp.concatenate([terms, jnp.zeros((queries - dims, queries), jnp.float32)], axis=0)
    share = jnp.sum(terms.T, axis=0, keepdims=True)
    for peer in range(share_ref.shape[0]):
        share_ref[peer] = share


def add_kernel(shares_ref, out_ref):
    total = tree_sum([shares_ref[peer] for peer in range(shares_ref.shape[0])])
    out_ref[...] = total[0, : out_ref.shape[0]]


def everyone(x, axis):
    size = lax.axis_size(axis)
    return [x] + [
        lax.ppermute(x, axis, [(i, i ^ offset) for i in range(size)]) for offset in range(1, size)
    ]


def call(kernel, args, outs, scratch=()):
    single = len(outs) == 1
    return pl.pallas_call(
        kernel,
        out_shape=outs[0] if single else outs,
        in_specs=[pl.BlockSpec(memory_space=pltpu.VMEM)] * len(args),
        out_specs=pl.BlockSpec(memory_space=pltpu.VMEM)
        if single
        else [pl.BlockSpec(memory_space=pltpu.VMEM)] * len(outs),
        scratch_shapes=list(scratch),
        compiler_params=pltpu.CompilerParams(vmem_limit_bytes=32 << 20),
    )(*args)


def shape(*sizes):
    return jax.ShapeDtypeStruct(sizes, jnp.float32)


def on_device(samples, bounds, spread, counts):
    dims, width = samples.shape
    queries = bounds.shape[2]
    blocks = lax.axis_size("blk")
    sample_total = width * blocks * lax.axis_size("grp")
    query_total = queries * blocks
    total = width * blocks

    spread, counts = spread.reshape(1, dims), counts.reshape(1, queries)
    packed, target = call(
        pack_kernel,
        [samples, bounds, spread, counts],
        [shape(blocks, 8, dims * width // 8), shape(1, queries)],
    )
    gathered = lax.all_to_all(packed, "blk", 0, 0)
    part = call(
        functools.partial(terms_kernel, width),
        [gathered, bounds, spread],
        [shape(dims + 8, queries)],
        [
            pltpu.VMEM((total, (LIMITED + 1) * queries), jnp.float32),
            pltpu.VMEM((total, 2 * queries), jnp.bfloat16),
        ],
    )
    parts = everyone(part, "grp")
    log_est, share = call(
        functools.partial(finish_kernel, sample_total, query_total),
        parts + [target],
        [shape(1, queries), shape(blocks, 1, queries)],
    )
    shares = lax.all_to_all(share, "blk", 0, 0)
    gradient = call(add_kernel, [shares], [shape(dims)])
    return log_est.reshape(queries), gradient


def solution(mesh):
    return jax.shard_map(
        on_device,
        mesh=mesh,
        in_specs=(P(None, ("blk", "grp")), P(None, None, "blk"), P(), P("blk")),
        out_specs=(P("blk"), P()),
        check_vma=False,
    )
```

profile of v0, /device:TPU:0, one launch (start us, length us, event | category | flops | bytes accessed | tf_op | source)
XLA Modules:
  0.0 32.3 jit_solution(2852785023607914076)
XLA Ops:
  0.6 0.0 copy-start.3
  0.6 0.0 copy-start.4
  0.6 0.6 %copy-done.3 = f32[32]{0:T(128)S(1)} copy-done((f32[32]{0:T(128)S(1)}, f32[32]{0:T(128)}, u32[]{:S(2)}) %copy-start.3) | copy-done | bytes 152
  1.3 0.0 copy-done.4
  1.3 0.0 copy-start
  1.3 0.8 %copy-done = s32[2,32,128]{2,1,0:T(8,128)S(1)} copy-done((s32[2,32,128]{2,1,0:T(8,128)S(1)}, s32[2,32,128]{2,1,0:T(8,128)}, u32[]{:S(2)}) %copy-start) | copy-done | bytes 32792
  2.1 0.0 copy-start.2
  2.1 0.7 %copy-done.2 = f32[32,32]{1,0:T(8,128)S(1)} copy-done((f32[32,32]{1,0:T(8,128)S(1)}, f32[32,32]{1,0:T(8,128)}, u32[]{:S(2)}) %copy-start.2) | copy-done | bytes 4120
  2.8 0.1 shard_map.59
  2.9 0.0 copy-start.1
  2.9 15.8 %all_to_all.10.blocks_ref = f32[16,8,128]{2,1,0:T(8,128)S(1)} all-to-all(f32[16,8,128]{2,1,0:T(8,128)S(1)} %get-tuple-element.6), channel_id=1, replica_groups=mesh['blk'=16,'grp'=2] {'blk'}, dimensions={0} | all-to-all | bytes 131072 | tf_op jit(solution)/shard_map/all_to_all | solution.py:199
  18.6 0.0 copy-done.1
  18.6 1.6 %shard_map.60.refs_0_ = f32[40,128]{1,0:T(8,128)S(1)} custom-call(f32[16,8,128]{2,1,0:T(8,128)S(1)} %all_to_all.10.blocks_ref, s32[2,32,128]{2,1,0:T(8,128)S(1)} %copy-done.1, f32[1,32]{1,0:T(1,128)S(1)} %bitcast.4), custom_call_target="tpu_custom_call" | custom-call | tf_op jit(solution)/shard_map/pallas_call | solution.py:169
  20.2 0.1 collective-permute-start
  20.3 1.2 %collective-permute-done.refs_1_ = f32[40,128]{1,0:T(8,128)S(1)} collective-permute-done((f32[40,128]{1,0:T(8,128)S(1)}, f32[40,128]{1,0:T(8,128)S(1)}, u32[]{:S(2)}, u32[]{:S(2)}) %collective-permute-start) | collective-permute-done | bytes 20512 | tf_op jit(solution)/shard_map/ppermute | solution.py:163
  21.5 0.5 %shard_map.61 = (f32[1,128]{1,0:T(1,128)}, f32[16,1,128]{2,1,0:T(1,128)S(1)}) custom-call(f32[40,128]{1,0:T(8,128)S(1)} %shard_map.60.refs_0_, f32[40,128]{1,0:T(8,128)S(1)} %collective-permute-done.refs_1_, f32[1,128]{1,0:T(1,128)S(1)} %get-tuple-element.7.refs_2_), custom_call_target="tpu_custom_call" | custom-call | tf_op jit(solution)/shard_map/pallas_call | solution.py:169
  22.0 9.8 %all_to_all.11.shares_ref = f32[16,1,128]{2,1,0:T(1,128)S(1)} all-to-all(f32[16,1,128]{2,1,0:T(1,128)S(1)} %get-tuple-element.9), channel_id=1, replica_groups=mesh['blk'=16,'grp'=2] {'blk'}, dimensions={0} | all-to-all | bytes 16384 | tf_op jit(solution)/shard_map/all_to_all | solution.py:215
  31.8 0.5 %shard_map.62 = f32[32]{0:T(128)} custom-call(f32[16,1,128]{2,1,0:T(1,128)S(1)} %all_to_all.11.shares_ref), custom_call_target="tpu_custom_call" | custom-call | tf_op jit(solution)/shard_map/pallas_call | solution.py:169
Async XLA Ops:
  0.6 0.7 %copy-start.3 = (f32[32]{0:T(128)S(1)}, f32[32]{0:T(128)}, u32[]{:S(2)}) copy-start(f32[32]{0:T(128)} %param.6) | copy-start | bytes 388
  0.6 0.7 %copy-start.4 = (s32[128]{0:T(128)S(1)}, s32[128]{0:T(128)}, u32[]{:S(2)}) copy-start(s32[128]{0:T(128)} %param.7) | copy-start | bytes 1540
  1.3 0.8 %copy-start = (s32[2,32,128]{2,1,0:T(8,128)S(1)}, s32[2,32,128]{2,1,0:T(8,128)}, u32[]{:S(2)}) copy-start(s32[2,32,128]{2,1,0:T(8,128)} %bounds_ref.3) | copy-start | bytes 98308
  2.1 0.7 %copy-start.2 = (f32[32,32]{1,0:T(8,128)S(1)}, f32[32,32]{1,0:T(8,128)}, u32[]{:S(2)}) copy-start(f32[32,32]{1,0:T(8,128)} %x_ref.1) | copy-start | bytes 12292
  2.9 15.8 %copy-start.1 = (s32[2,32,128]{2,1,0:T(8,128)S(1)}, s32[2,32,128]{2,1,0:T(8,128)}, u32[]{:S(2)}) copy-start(s32[2,32,128]{2,1,0:T(8,128)} %bounds_ref.3) | copy-start | bytes 98308
  20.2 1.3 %collective-permute-start = (f32[40,128]{1,0:T(8,128)S(1)}, f32[40,128]{1,0:T(8,128)S(1)}, u32[]{:S(2)}, u32[]{:S(2)}) collective-permute-start(f32[40,128]{1,0:T(8,128)S(1)} %shard_map.60.refs_0_), channel_id=1, source_target_pairs={{0,1},{1,0},{2,3},{3,2},{4,5},{5,4},{6,7},{7,6},{8,9},{9,8},{10,11... | collective-permute-start | bytes 61448 | tf_op jit(solution)/shard_map/ppermute | solution.py:163
where the time goes:
time: 32.7 us; the launch traced here: 32.3 us
  blocking collectives  25.6 us (78%)
  Pallas kernels  2.68 us (8%)
  local copies, waits for them, and re-layouts  2.13 us (7%)
  waiting for transfers between devices  1.18 us (4%)
  between operations  0.67 us (2%)
    all_to_all x1, blocking collectives, on_device(): gathered = lax.all_to_all(packed, 'blk', 0, 0)  15.8 us
    all_to_all x1, blocking collectives, on_device(): shares = lax.all_to_all(share, 'blk', 0, 0)  9.84 us
    pallas_call x4, Pallas kernels, call(): pl.pallas_call(kernel, out_shape=outs[0] if single else outs, in_specs=[p...  2.68 us
    unnamed x10, local copies, waits for them, and re-layouts  2.13 us
    ppermute x1, waiting for transfers between devices, everyone(): lax.ppermute(x, axis, [(i, i ^ offset) for i in range(size)])  1.18 us
  transfers between devices with their start and end apart: 1, of which 1 were waited for; matrix products, arithmetic and copies ran while one was open for 0% of the time, Pallas kernels for 0%

commit v1 on v0

--- a/solution.py
+++ b/solution.py
@@ -1,4 +1,5 @@
 import functools
+import math
 
 import jax
 import jax.numpy as jnp
@@ -36,19 +37,28 @@
     return out + [x.astype(jnp.bfloat16)]
 
 
-def tree_sum(parts):
-    while len(parts) > 1:
-        parts = [a + b for a, b in zip(parts[::2], parts[1::2])]
-    return parts[0]
-
-
-def pack_kernel(x_ref, bounds_ref, spread_ref, counts_ref, out_ref, target_ref):
-    rows, width = x_ref.shape
-    packed = jnp.concatenate([x_ref[8 * j : 8 * (j + 1), :] for j in range(rows // 8)], axis=1)
+def load_kernel(
+    x_ref, bounds_ref, spread_ref, counts_ref,
+    out_ref, held_bounds, held_spread, target_ref,
+    held_x, held_counts, sems,
+):
+    sources = (x_ref, bounds_ref, spread_ref, counts_ref)
+    targets = (held_x, held_bounds, held_spread, held_counts)
+    copies = [
+        pltpu.make_async_copy(source, target, sems.at[i])
+        for i, (source, target) in enumerate(zip(sources, targets))
+    ]
+    for copy in copies:
+        copy.start()
+    copies[0].wait()
+    rows = held_x.shape[0]
+    packed = jnp.concatenate([held_x[8 * j : 8 * (j + 1), :] for j in range(rows // 8)], axis=1)
     for peer in range(out_ref.shape[0]):
         out_ref[peer] = packed
+    for copy in copies[1:]:
+        copy.wait()
     smoothing = 1.0 / TABLE_ROWS
-    target_ref[...] = jnp.log(counts_ref[...].astype(jnp.float32) / TABLE_ROWS + smoothing)
+    target_ref[...] = jnp.log(held_counts[...].astype(jnp.float32) / TABLE_ROWS + smoothing)
 
 
 def terms_kernel(width, blocks_ref, bounds_ref, spread_ref, out_ref, picked, inside):
@@ -138,38 +148,65 @@
 
 def finish_kernel(sample_total, query_total, *refs):
     part_refs, (target_ref, log_ref, share_ref) = refs[:-3], refs[-3:]
-    whole = tree_sum([ref[...] for ref in part_refs])
+    whole = total_of(part_refs)
     dims, queries = whole.shape[0] - 8, whole.shape[1]
     smoothing = 1.0 / TABLE_ROWS
     estimate = whole[dims : dims + 1] / sample_total
     log_est = jnp.log(estimate + smoothing)
-    log_ref[...] = log_est
+    leads = lax.axis_index("grp") == lax.axis_size("grp") - 1
+    log_ref[...] = jnp.where(leads, log_est, 0.0)
     weight = 2.0 * (log_est - target_ref[...]) / (query_total * (estimate + smoothing))
     terms = whole[:dims] * (weight / sample_total)
     terms = jnp.concatenate([terms, jnp.zeros((queries - dims, queries), jnp.float32)], axis=0)
-    share = jnp.sum(terms.T, axis=0, keepdims=True)
-    for peer in range(share_ref.shape[0]):
-        share_ref[peer] = share
-
-
-def add_kernel(shares_ref, out_ref):
-    total = tree_sum([shares_ref[peer] for peer in range(shares_ref.shape[0])])
-    out_ref[...] = total[0, : out_ref.shape[0]]
-
-
-def everyone(x, axis):
-    size = lax.axis_size(axis)
-    return [x] + [
-        lax.ppermute(x, axis, [(i, i ^ offset) for i in range(size)]) for offset in range(1, size)
-    ]
-
-
-def call(kernel, args, outs, scratch=()):
+    share_ref[...] = jnp.sum(terms.T, axis=0, keepdims=True)
+
+
+def total_of(refs):
+    total = refs[0][...]
+    for ref in refs[1:]:
+        total = total + ref[...]
+    return total
+
+
+def sum_kernel(*refs):
+    refs[-1][...] = total_of(refs[:-1])
+
+
+def root_kernel(*refs):
+    *shares, log_ref, total_ref, both_ref = refs
+    leads = lax.axis_index("grp") == lax.axis_size("grp") - 1
+    root = leads & (lax.axis_index("blk") == 0)
+    total = jnp.where(root, total_of(shares), 0.0)
+    total_ref[...] = total
+    both_ref[:1, :] = total
+    both_ref[1:, :] = log_ref[...]
+
+
+def spread_kernel(*refs):
+    *shares, pair_ref, total_ref, held_ref = refs
+    total_ref[...] = total_of(shares)
+    held_ref[...] = pair_ref[...]
+
+
+def pair_kernel(*refs):
+    *shares, log_ref, both_ref = refs
+    both_ref[:1, :] = total_of(shares)
+    both_ref[1:, :] = log_ref[...]
+
+
+def last_kernel(*refs):
+    *both, log_ref, gradient_ref = refs
+    total = total_of(both)
+    log_ref[...] = total[1]
+    gradient_ref[...] = total[0, : gradient_ref.shape[0]]
+
+
+def call(kernel, args, outs, scratch=(), placed=pltpu.VMEM):
     single = len(outs) == 1
     return pl.pallas_call(
         kernel,
         out_shape=outs[0] if single else outs,
-        in_specs=[pl.BlockSpec(memory_space=pltpu.VMEM)] * len(args),
+        in_specs=[pl.BlockSpec(memory_space=placed)] * len(args),
         out_specs=pl.BlockSpec(memory_space=pltpu.VMEM)
         if single
         else [pl.BlockSpec(memory_space=pltpu.VMEM)] * len(outs),
@@ -185,16 +222,33 @@
 def on_device(samples, bounds, spread, counts):
     dims, width = samples.shape
     queries = bounds.shape[2]
-    blocks = lax.axis_size("blk")
-    sample_total = width * blocks * lax.axis_size("grp")
+    blocks, copies = lax.axis_size("blk"), lax.axis_size("grp")
+    sample_total = width * blocks * copies
     query_total = queries * blocks
     total = width * blocks
 
-    spread, counts = spread.reshape(1, dims), counts.reshape(1, queries)
-    packed, target = call(
-        pack_kernel,
-        [samples, bounds, spread, counts],
-        [shape(blocks, 8, dims * width // 8), shape(1, queries)],
+    both = ("blk", "grp")
+    lead = lambda block: block * copies + copies - 1
+    send = lambda x, pairs: lax.ppermute(x, both, pairs)
+    size = math.isqrt(blocks)
+    groups = [list(range(b, min(b + size, blocks))) for b in range(1, blocks, size)]
+    followers = [[(g[0], g[m]) for g in groups if len(g) > m] for m in range(1, size)]
+
+    counts_vector = pltpu.VMEM((1, queries), jnp.int32)
+    packed, bounds, spread, target = call(
+        load_kernel,
+        [
+            pltpu.with_memory_space_constraint(array, pltpu.HBM)
+            for array in (samples, bounds, spread.reshape(1, dims), counts.reshape(1, queries))
+        ],
+        [
+            pltpu.VMEM((blocks, 8, dims * width // 8), jnp.float32),
+            pltpu.VMEM(bounds.shape, bounds.dtype),
+            pltpu.VMEM((1, dims), jnp.float32),
+            pltpu.VMEM((1, queries), jnp.float32),
+        ],
+        [pltpu.VMEM((dims, width), jnp.float32), counts_vector, pltpu.SemaphoreType.DMA((4,))],
+        placed=pl.ANY,
     )
     gathered = lax.all_to_all(packed, "blk", 0, 0)
     part = call(
@@ -206,15 +260,38 @@
             pltpu.VMEM((total, 2 * queries), jnp.bfloat16),
         ],
     )
-    parts = everyone(part, "grp")
+    parts = [part] + [
+        send(part, [(b * copies + c, lead(b)) for b in range(blocks)]) for c in range(copies - 1)
+    ]
     log_est, share = call(
         functools.partial(finish_kernel, sample_total, query_total),
         parts + [target],
-        [shape(1, queries), shape(blocks, 1, queries)],
-    )
-    shares = lax.all_to_all(share, "blk", 0, 0)
-    gradient = call(add_kernel, [shares], [shape(dims)])
-    return log_est.reshape(queries), gradient
+        [shape(1, queries), shape(1, queries)],
+    )
+
+    row = shape(1, queries)
+    shares = [share] + [
+        send(share, [(lead(follower), lead(leader)) for leader, follower in pairs])
+        for pairs in followers
+    ]
+    share = call(sum_kernel, shares, [row])
+    shares = [share] + [send(share, [(lead(g[0]), lead(0))]) for g in groups]
+    share, pair = call(root_kernel, shares + [log_est], [row, shape(2, queries)])
+    shares = [share] + [send(share, [(lead(0), lead(g[0]))]) for g in groups]
+    at_root = functools.reduce(
+        jnp.add, [send(pair, [(lead(0), c)]) for c in range(copies - 1)]
+    )
+    share, at_root = call(spread_kernel, shares + [at_root], [row, shape(2, queries)])
+    shares = [share] + [
+        send(share, [(lead(leader), lead(follower)) for leader, follower in pairs])
+        for pairs in followers
+    ]
+    pair = call(pair_kernel, shares + [log_est], [shape(2, queries)])
+    elsewhere = [
+        send(pair, [(lead(b), b * copies + c) for b in range(1, blocks)]) for c in range(copies - 1)
+    ]
+    log_est, gradient = call(last_kernel, [pair, at_root] + elsewhere, [shape(queries), shape(dims)])
+    return log_est, gradient
 
 
 def solution(mesh):

time: 32.7 us -> 49.2 us (1.50)
  the two profiles are of different devices: /device:TPU:0 before, /device:TPU:5 now
where the time goes in v1:
time: 49.2 us; the launch traced here: 48.8 us
  starting transfers between devices  17 us (35%)
  waiting for transfers between devices  15.9 us (32%)
  blocking collectives  11.9 us (24%)
  Pallas kernels  3.08 us (6%)
  between operations  0.91 us (2%)
    ppermute x17, starting transfers between devices, on_device(): send = lambda x, pairs: lax.ppermute(x, both, pairs)  17 us
    ppermute x17, waiting for transfers between devices, on_device(): send = lambda x, pairs: lax.ppermute(x, both, pairs)  15.9 us
    all_to_all x1, blocking collectives, on_device(): gathered = lax.all_to_all(packed, 'blk', 0, 0)  11.9 us
    pallas_call x8, Pallas kernels, call(): pl.pallas_call(kernel, out_shape=outs[0] if single else outs, in_specs=[p...  3.08 us
  transfers between devices with their start and end apart: 17, of which 4 were waited for; matrix products, arithmetic and copies ran while one was open for 0% of the time, Pallas kernels for 0%

profile of v1, /device:TPU:5, one launch (start us, length us, event | category | flops | bytes accessed | tf_op | source)
XLA Modules:
  0.0 48.8 jit_solution(11307573575605157120)
XLA Ops:
  0.6 0.8 %shard_map.59 = (f32[16,8,128]{2,1,0:T(8,128)S(1)}, s32[2,32,128]{2,1,0:T(8,128)S(1)}, f32[1,32]{1,0:T(1,128)S(1)}, f32[1,128]{1,0:T(1,128)S(1)}) custom-call(f32[32,32]{1,0:T(8,128)} %x_ref.1, s32[2,32,128]{2,1,0:T(8,128)} %bounds_ref.1, f32[1,32]{1,0:T(1,128)} %bitcast.2, s32[1,128]{1,0:T(1,128)} %bitcast.3), custom_call_target="tpu_custom_call" | custom-call | tf_op jit(solution)/shard_map/pallas_call | solution.py:206
  1.5 11.9 %all_to_all.5.blocks_ref = f32[16,8,128]{2,1,0:T(8,128)S(1)} all-to-all(f32[16,8,128]{2,1,0:T(8,128)S(1)} %get-tuple-element.12), channel_id=1, replica_groups=mesh['blk'=16,'grp'=2] {'blk'}, dimensions={0} | all-to-all | bytes 131072 | tf_op jit(solution)/shard_map/all_to_all | solution.py:253
  13.4 1.6 %shard_map.60.refs_0_ = f32[40,128]{1,0:T(8,128)S(1)} custom-call(f32[16,8,128]{2,1,0:T(8,128)S(1)} %all_to_all.5.blocks_ref, s32[2,32,128]{2,1,0:T(8,128)S(1)} %get-tuple-element.13.bounds_ref, f32[1,32]{1,0:T(1,128)S(1)} %get-tuple-element.14.spread_ref), custom_call_target="tpu_custom_call" | custom-call | tf_op jit(solution)/shard_map/pallas_call | solution.py:206
  15.0 1.3 %collective-permute-start = (f32[40,128]{1,0:T(8,128)S(1)}, f32[40,128]{1,0:T(8,128)S(1)}, u32[]{:S(2)}, u32[]{:S(2)}) collective-permute-start(f32[40,128]{1,0:T(8,128)S(1)} %shard_map.60.refs_0_), channel_id=1, source_target_pairs={{0,1},{2,3},{4,5},{6,7},{8,9},{10,11},{12,13},{14,15},{16,17},{18,... | collective-permute-start | bytes 61448 | tf_op jit(solution)/shard_map/ppermute | solution.py:232
  16.3 2.8 %collective-permute-done.refs_1_ = f32[40,128]{1,0:T(8,128)S(1)} collective-permute-done((f32[40,128]{1,0:T(8,128)S(1)}, f32[40,128]{1,0:T(8,128)S(1)}, u32[]{:S(2)}, u32[]{:S(2)}) %collective-permute-start) | collective-permute-done | bytes 20512 | tf_op jit(solution)/shard_map/ppermute | solution.py:232
  19.1 0.7 %collective-permute-start.3 = (f32[1,128]{1,0:T(1,128)S(1)}, f32[1,128]{1,0:T(1,128)S(1)}, u32[]{:S(2)}, u32[]{:S(2)}) collective-permute-start(f32[1,128]{1,0:T(1,128)S(1)} %get-tuple-element.16.refs_0_), channel_id=1, source_target_pairs={{9,3},{17,11},{25,19}} | collective-permute-start | bytes 1544 | tf_op jit(solution)/shard_map/ppermute | solution.py:232
  19.8 0.7 %collective-permute-start.2 = (f32[1,128]{1,0:T(1,128)S(1)}, f32[1,128]{1,0:T(1,128)S(1)}, u32[]{:S(2)}, u32[]{:S(2)}) collective-permute-start(f32[1,128]{1,0:T(1,128)S(1)} %get-tuple-element.16.refs_0_), channel_id=1, source_target_pairs={{7,3},{15,11},{23,19},{31,27}} | collective-permute-start | bytes 1544 | tf_op jit(solution)/shard_map/ppermute | solution.py:232
  20.5 4.5 %collective-permute-start.1 = (f32[1,128]{1,0:T(1,128)S(1)}, f32[1,128]{1,0:T(1,128)S(1)}, u32[]{:S(2)}, u32[]{:S(2)}) collective-permute-start(f32[1,128]{1,0:T(1,128)S(1)} %get-tuple-element.16.refs_0_), channel_id=1, source_target_pairs={{5,3},{13,11},{21,19},{29,27}} | collective-permute-start | bytes 1544 | tf_op jit(solution)/shard_map/ppermute | solution.py:232
  25.0 0.7 %collective-permute-done.1.refs_1_ = f32[1,128]{1,0:T(1,128)S(1)} collective-permute-done((f32[1,128]{1,0:T(1,128)S(1)}, f32[1,128]{1,0:T(1,128)S(1)}, u32[]{:S(2)}, u32[]{:S(2)}) %collective-permute-start.1) | collective-permute-done | bytes 544 | tf_op jit(solution)/shard_map/ppermute | solution.py:232
  25.7 0.6 %collective-permute-start.7 = (f32[1,128]{1,0:T(1,128)S(1)}, f32[1,128]{1,0:T(1,128)S(1)}, u32[]{:S(2)}, u32[]{:S(2)}) collective-permute-start(f32[1,128]{1,0:T(1,128)S(1)} %shard_map.62.refs_0_), channel_id=1, source_target_pairs={{27,1}} | collective-permute-start | bytes 1544 | tf_op jit(solution)/shard_map/ppermute | solution.py:232
  26.4 0.7 %collective-permute-start.6 = (f32[1,128]{1,0:T(1,128)S(1)}, f32[1,128]{1,0:T(1,128)S(1)}, u32[]{:S(2)}, u32[]{:S(2)}) collective-permute-start(f32[1,128]{1,0:T(1,128)S(1)} %shard_map.62.refs_0_), channel_id=1, source_target_pairs={{19,1}} | collective-permute-start | bytes 1544 | tf_op jit(solution)/shard_map/ppermute | solution.py:232
  27.0 0.7 %collective-permute-start.5 = (f32[1,128]{1,0:T(1,128)S(1)}, f32[1,128]{1,0:T(1,128)S(1)}, u32[]{:S(2)}, u32[]{:S(2)}) collective-permute-start(f32[1,128]{1,0:T(1,128)S(1)} %shard_map.62.refs_0_), channel_id=1, source_target_pairs={{11,1}} | collective-permute-start | bytes 1544 | tf_op jit(solution)/shard_map/ppermute | solution.py:232
  27.7 0.7 %collective-permute-start.4 = (f32[1,128]{1,0:T(1,128)S(1)}, f32[1,128]{1,0:T(1,128)S(1)}, u32[]{:S(2)}, u32[]{:S(2)}) collective-permute-start(f32[1,128]{1,0:T(1,128)S(1)} %shard_map.62.refs_0_), channel_id=1, source_target_pairs={{3,1}} | collective-permute-start | bytes 1544 | tf_op jit(solution)/shard_map/ppermute | solution.py:232
  28.4 0.7 %collective-permute-start.12 = (f32[2,128]{1,0:T(2,128)S(1)}, f32[2,128]{1,0:T(2,128)S(1)}, u32[]{:S(2)}, u32[]{:S(2)}) collective-permute-start(f32[2,128]{1,0:T(2,128)S(1)} %get-tuple-element.19), channel_id=1, source_target_pairs={{1,0}} | collective-permute-start | bytes 3080 | tf_op jit(solution)/shard_map/ppermute | solution.py:232
  29.1 0.7 %collective-permute-start.11 = (f32[1,128]{1,0:T(1,128)S(1)}, f32[1,128]{1,0:T(1,128)S(1)}, u32[]{:S(2)}, u32[]{:S(2)}) collective-permute-start(f32[1,128]{1,0:T(1,128)S(1)} %get-tuple-element.18.refs_0_), channel_id=1, source_target_pairs={{1,27}} | collective-permute-start | bytes 1544 | tf_op jit(solution)/shard_map/ppermute | solution.py:232
  29.8 0.7 %collective-permute-start.10 = (f32[1,128]{1,0:T(1,128)S(1)}, f32[1,128]{1,0:T(1,128)S(1)}, u32[]{:S(2)}, u32[]{:S(2)}) collective-permute-start(f32[1,128]{1,0:T(1,128)S(1)} %get-tuple-element.18.refs_0_), channel_id=1, source_target_pairs={{1,19}} | collective-permute-start | bytes 1544 | tf_op jit(solution)/shard_map/ppermute | solution.py:232
  30.5 0.7 %collective-permute-start.9 = (f32[1,128]{1,0:T(1,128)S(1)}, f32[1,128]{1,0:T(1,128)S(1)}, u32[]{:S(2)}, u32[]{:S(2)}) collective-permute-start(f32[1,128]{1,0:T(1,128)S(1)} %get-tuple-element.18.refs_0_), channel_id=1, source_target_pairs={{1,11}} | collective-permute-start | bytes 1544 | tf_op jit(solution)/shard_map/ppermute | solution.py:232
  31.1 0.7 %collective-permute-start.8 = (f32[1,128]{1,0:T(1,128)S(1)}, f32[1,128]{1,0:T(1,128)S(1)}, u32[]{:S(2)}, u32[]{:S(2)}) collective-permute-start(f32[1,128]{1,0:T(1,128)S(1)} %get-tuple-element.18.refs_0_), channel_id=1, source_target_pairs={{1,3}} | collective-permute-start | bytes 1544 | tf_op jit(solution)/shard_map/ppermute | solution.py:232
  31.9 0.7 %collective-permute-start.15 = (f32[1,128]{1,0:T(1,128)S(1)}, f32[1,128]{1,0:T(1,128)S(1)}, u32[]{:S(2)}, u32[]{:S(2)}) collective-permute-start(f32[1,128]{1,0:T(1,128)S(1)} %get-tuple-element.20.refs_0_), channel_id=1, source_target_pairs={{3,9},{11,17},{19,25}} | collective-permute-start | bytes 1544 | tf_op jit(solution)/shard_map/ppermute | solution.py:232
  32.5 0.7 %collective-permute-start.14 = (f32[1,128]{1,0:T(1,128)S(1)}, f32[1,128]{1,0:T(1,128)S(1)}, u32[]{:S(2)}, u32[]{:S(2)}) collective-permute-start(f32[1,128]{1,0:T(1,128)S(1)} %get-tuple-element.20.refs_0_), channel_id=1, source_target_pairs={{3,7},{11,15},{19,23},{27,31}} | collective-permute-start | bytes 1544 | tf_op jit(solution)/shard_map/ppermute | solution.py:232
  33.2 1.3 %collective-permute-start.13 = (f32[1,128]{1,0:T(1,128)S(1)}, f32[1,128]{1,0:T(1,128)S(1)}, u32[]{:S(2)}, u32[]{:S(2)}) collective-permute-start(f32[1,128]{1,0:T(1,128)S(1)} %get-tuple-element.20.refs_0_), channel_id=1, source_target_pairs={{3,5},{11,13},{19,21},{27,29}} | collective-permute-start | bytes 1544 | tf_op jit(solution)/shard_map/ppermute | solution.py:232
  34.5 11.6 %collective-permute-done.13.refs_1_ = f32[1,128]{1,0:T(1,128)S(1)} collective-permute-done((f32[1,128]{1,0:T(1,128)S(1)}, f32[1,128]{1,0:T(1,128)S(1)}, u32[]{:S(2)}, u32[]{:S(2)}) %collective-permute-start.13) | collective-permute-done | bytes 544 | tf_op jit(solution)/shard_map/ppermute | solution.py:232
  46.2 1.3 %collective-permute-start.16 = (f32[2,128]{1,0:T(2,128)S(1)}, f32[2,128]{1,0:T(2,128)S(1)}, u32[]{:S(2)}, u32[]{:S(2)}) collective-permute-start(f32[2,128]{1,0:T(2,128)S(1)} %shard_map.65.refs_0_), channel_id=1, source_target_pairs={{3,2},{5,4},{7,6},{9,8},{11,10},{13,12},{15,14},{17,16},{19,18},{2... | collective-permute-start | bytes 3080 | tf_op jit(solution)/shard_map/ppermute | solution.py:232
  47.5 0.8 %collective-permute-done.16.refs_2_ = f32[2,128]{1,0:T(2,128)S(1)} collective-permute-done((f32[2,128]{1,0:T(2,128)S(1)}, f32[2,128]{1,0:T(2,128)S(1)}, u32[]{:S(2)}, u32[]{:S(2)}) %collective-permute-start.16) | collective-permute-done | bytes 1056 | tf_op jit(solution)/shard_map/ppermute | solution.py:232
  (19 shorter events, 0.7 us)
Async XLA Ops:
  15.0 4.1 %collective-permute-start = (f32[40,128]{1,0:T(8,128)S(1)}, f32[40,128]{1,0:T(8,128)S(1)}, u32[]{:S(2)}, u32[]{:S(2)}) collective-permute-start(f32[40,128]{1,0:T(8,128)S(1)} %shard_map.60.refs_0_), channel_id=1, source_target_pairs={{0,1},{2,3},{4,5},{6,7},{8,9},{10,11},{12,13},{14,15},{16,17},{18,... | collective-permute-start | bytes 61448 | tf_op jit(solution)/shard_map/ppermute | solution.py:232
  19.1 5.9 %collective-permute-start.3 = (f32[1,128]{1,0:T(1,128)S(1)}, f32[1,128]{1,0:T(1,128)S(1)}, u32[]{:S(2)}, u32[]{:S(2)}) collective-permute-start(f32[1,128]{1,0:T(1,128)S(1)} %get-tuple-element.16.refs_0_), channel_id=1, source_target_pairs={{9,3},{17,11},{25,19}} | collective-permute-start | bytes 1544 | tf_op jit(solution)/shard_map/ppermute | solution.py:232
  19.8 5.2 %collective-permute-start.2 = (f32[1,128]{1,0:T(1,128)S(1)}, f32[1,128]{1,0:T(1,128)S(1)}, u32[]{:S(2)}, u32[]{:S(2)}) collective-permute-start(f32[1,128]{1,0:T(1,128)S(1)} %get-tuple-element.16.refs_0_), channel_id=1, source_target_pairs={{7,3},{15,11},{23,19},{31,27}} | collective-permute-start | bytes 1544 | tf_op jit(solution)/shard_map/ppermute | solution.py:232
  20.5 5.2 %collective-permute-start.1 = (f32[1,128]{1,0:T(1,128)S(1)}, f32[1,128]{1,0:T(1,128)S(1)}, u32[]{:S(2)}, u32[]{:S(2)}) collective-permute-start(f32[1,128]{1,0:T(1,128)S(1)} %get-tuple-element.16.refs_0_), channel_id=1, source_target_pairs={{5,3},{13,11},{21,19},{29,27}} | collective-permute-start | bytes 1544 | tf_op jit(solution)/shard_map/ppermute | solution.py:232
  25.7 2.7 %collective-permute-start.7 = (f32[1,128]{1,0:T(1,128)S(1)}, f32[1,128]{1,0:T(1,128)S(1)}, u32[]{:S(2)}, u32[]{:S(2)}) collective-permute-start(f32[1,128]{1,0:T(1,128)S(1)} %shard_map.62.refs_0_), channel_id=1, source_target_pairs={{27,1}} | collective-permute-start | bytes 1544 | tf_op jit(solution)/shard_map/ppermute | solution.py:232
  26.4 2.0 %collective-permute-start.6 = (f32[1,128]{1,0:T(1,128)S(1)}, f32[1,128]{1,0:T(1,128)S(1)}, u32[]{:S(2)}, u32[]{:S(2)}) collective-permute-start(f32[1,128]{1,0:T(1,128)S(1)} %shard_map.62.refs_0_), channel_id=1, source_target_pairs={{19,1}} | collective-permute-start | bytes 1544 | tf_op jit(solution)/shard_map/ppermute | solution.py:232
  27.0 1.4 %collective-permute-start.5 = (f32[1,128]{1,0:T(1,128)S(1)}, f32[1,128]{1,0:T(1,128)S(1)}, u32[]{:S(2)}, u32[]{:S(2)}) collective-permute-start(f32[1,128]{1,0:T(1,128)S(1)} %shard_map.62.refs_0_), channel_id=1, source_target_pairs={{11,1}} | collective-permute-start | bytes 1544 | tf_op jit(solution)/shard_map/ppermute | solution.py:232
  27.7 0.7 %collective-permute-start.4 = (f32[1,128]{1,0:T(1,128)S(1)}, f32[1,128]{1,0:T(1,128)S(1)}, u32[]{:S(2)}, u32[]{:S(2)}) collective-permute-start(f32[1,128]{1,0:T(1,128)S(1)} %shard_map.62.refs_0_), channel_id=1, source_target_pairs={{3,1}} | collective-permute-start | bytes 1544 | tf_op jit(solution)/shard_map/ppermute | solution.py:232
  28.4 3.4 %collective-permute-start.12 = (f32[2,128]{1,0:T(2,128)S(1)}, f32[2,128]{1,0:T(2,128)S(1)}, u32[]{:S(2)}, u32[]{:S(2)}) collective-permute-start(f32[2,128]{1,0:T(2,128)S(1)} %get-tuple-element.19), channel_id=1, source_target_pairs={{1,0}} | collective-permute-start | bytes 3080 | tf_op jit(solution)/shard_map/ppermute | solution.py:232
  29.1 2.7 %collective-permute-start.11 = (f32[1,128]{1,0:T(1,128)S(1)}, f32[1,128]{1,0:T(1,128)S(1)}, u32[]{:S(2)}, u32[]{:S(2)}) collective-permute-start(f32[1,128]{1,0:T(1,128)S(1)} %get-tuple-element.18.refs_0_), channel_id=1, source_target_pairs={{1,27}} | collective-permute-start | bytes 1544 | tf_op jit(solution)/shard_map/ppermute | solution.py:232
  29.8 2.0 %collective-permute-start.10 = (f32[1,128]{1,0:T(1,128)S(1)}, f32[1,128]{1,0:T(1,128)S(1)}, u32[]{:S(2)}, u32[]{:S(2)}) collective-permute-start(f32[1,128]{1,0:T(1,128)S(1)} %get-tuple-element.18.refs_0_), channel_id=1, source_target_pairs={{1,19}} | collective-permute-start | bytes 1544 | tf_op jit(solution)/shard_map/ppermute | solution.py:232
  30.5 1.4 %collective-permute-start.9 = (f32[1,128]{1,0:T(1,128)S(1)}, f32[1,128]{1,0:T(1,128)S(1)}, u32[]{:S(2)}, u32[]{:S(2)}) collective-permute-start(f32[1,128]{1,0:T(1,128)S(1)} %get-tuple-element.18.refs_0_), channel_id=1, source_target_pairs={{1,11}} | collective-permute-start | bytes 1544 | tf_op jit(solution)/shard_map/ppermute | solution.py:232
  31.1 0.7 %collective-permute-start.8 = (f32[1,128]{1,0:T(1,128)S(1)}, f32[1,128]{1,0:T(1,128)S(1)}, u32[]{:S(2)}, u32[]{:S(2)}) collective-permute-start(f32[1,128]{1,0:T(1,128)S(1)} %get-tuple-element.18.refs_0_), channel_id=1, source_target_pairs={{1,3}} | collective-permute-start | bytes 1544 | tf_op jit(solution)/shard_map/ppermute | solution.py:232
  31.9 2.6 %collective-permute-start.15 = (f32[1,128]{1,0:T(1,128)S(1)}, f32[1,128]{1,0:T(1,128)S(1)}, u32[]{:S(2)}, u32[]{:S(2)}) collective-permute-start(f32[1,128]{1,0:T(1,128)S(1)} %get-tuple-element.20.refs_0_), channel_id=1, source_target_pairs={{3,9},{11,17},{19,25}} | collective-permute-start | bytes 1544 | tf_op jit(solution)/shard_map/ppermute | solution.py:232
  32.5 2.0 %collective-permute-start.14 = (f32[1,128]{1,0:T(1,128)S(1)}, f32[1,128]{1,0:T(1,128)S(1)}, u32[]{:S(2)}, u32[]{:S(2)}) collective-permute-start(f32[1,128]{1,0:T(1,128)S(1)} %get-tuple-element.20.refs_0_), channel_id=1, source_target_pairs={{3,7},{11,15},{19,23},{27,31}} | collective-permute-start | bytes 1544 | tf_op jit(solution)/shard_map/ppermute | solution.py:232
  33.2 13.0 %collective-permute-start.13 = (f32[1,128]{1,0:T(1,128)S(1)}, f32[1,128]{1,0:T(1,128)S(1)}, u32[]{:S(2)}, u32[]{:S(2)}) collective-permute-start(f32[1,128]{1,0:T(1,128)S(1)} %get-tuple-element.20.refs_0_), channel_id=1, source_target_pairs={{3,5},{11,13},{19,21},{27,29}} | collective-permute-start | bytes 1544 | tf_op jit(solution)/shard_map/ppermute | solution.py:232
  46.2 2.1 %collective-permute-start.16 = (f32[2,128]{1,0:T(2,128)S(1)}, f32[2,128]{1,0:T(2,128)S(1)}, u32[]{:S(2)}, u32[]{:S(2)}) collective-permute-start(f32[2,128]{1,0:T(2,128)S(1)} %shard_map.65.refs_0_), channel_id=1, source_target_pairs={{3,2},{5,4},{7,6},{9,8},{11,10},{13,12},{15,14},{17,16},{19,18},{2... | collective-permute-start | bytes 3080 | tf_op jit(solution)/shard_map/ppermute | solution.py:232

commit v2 on v0

--- a/solution.py
+++ b/solution.py
@@ -42,13 +42,28 @@
     return parts[0]
 
 
-def pack_kernel(x_ref, bounds_ref, spread_ref, counts_ref, out_ref, target_ref):
-    rows, width = x_ref.shape
-    packed = jnp.concatenate([x_ref[8 * j : 8 * (j + 1), :] for j in range(rows // 8)], axis=1)
+def load_kernel(
+    x_ref, bounds_ref, spread_ref, counts_ref,
+    out_ref, held_bounds, held_spread, target_ref,
+    held_x, held_counts, sems,
+):
+    sources = (x_ref, bounds_ref, spread_ref, counts_ref)
+    targets = (held_x, held_bounds, held_spread, held_counts)
+    copies = [
+        pltpu.make_async_copy(source, target, sems.at[i])
+        for i, (source, target) in enumerate(zip(sources, targets))
+    ]
+    for copy in copies:
+        copy.start()
+    copies[0].wait()
+    rows = held_x.shape[0]
+    packed = jnp.concatenate([held_x[8 * j : 8 * (j + 1), :] for j in range(rows // 8)], axis=1)
     for peer in range(out_ref.shape[0]):
         out_ref[peer] = packed
+    for copy in copies[1:]:
+        copy.wait()
     smoothing = 1.0 / TABLE_ROWS
-    target_ref[...] = jnp.log(counts_ref[...].astype(jnp.float32) / TABLE_ROWS + smoothing)
+    target_ref[...] = jnp.log(held_counts[...].astype(jnp.float32) / TABLE_ROWS + smoothing)
 
 
 def terms_kernel(width, blocks_ref, bounds_ref, spread_ref, out_ref, picked, inside):
@@ -152,9 +167,10 @@
         share_ref[peer] = share
 
 
-def add_kernel(shares_ref, out_ref):
+def last_kernel(shares_ref, held_log_ref, log_ref, gradient_ref):
     total = tree_sum([shares_ref[peer] for peer in range(shares_ref.shape[0])])
-    out_ref[...] = total[0, : out_ref.shape[0]]
+    log_ref[...] = held_log_ref[0]
+    gradient_ref[...] = total[0, : gradient_ref.shape[0]]
 
 
 def everyone(x, axis):
@@ -164,12 +180,12 @@
     ]
 
 
-def call(kernel, args, outs, scratch=()):
+def call(kernel, args, outs, scratch=(), placed=pltpu.VMEM):
     single = len(outs) == 1
     return pl.pallas_call(
         kernel,
         out_shape=outs[0] if single else outs,
-        in_specs=[pl.BlockSpec(memory_space=pltpu.VMEM)] * len(args),
+        in_specs=[pl.BlockSpec(memory_space=placed)] * len(args),
         out_specs=pl.BlockSpec(memory_space=pltpu.VMEM)
         if single
         else [pl.BlockSpec(memory_space=pltpu.VMEM)] * len(outs),
@@ -185,18 +201,30 @@
 def on_device(samples, bounds, spread, counts):
     dims, width = samples.shape
     queries = bounds.shape[2]
-    blocks = lax.axis_size("blk")
-    sample_total = width * blocks * lax.axis_size("grp")
+    blocks, copies = lax.axis_size("blk"), lax.axis_size("grp")
+    sample_total = width * blocks * copies
     query_total = queries * blocks
     total = width * blocks
 
-    spread, counts = spread.reshape(1, dims), counts.reshape(1, queries)
-    packed, target = call(
-        pack_kernel,
-        [samples, bounds, spread, counts],
-        [shape(blocks, 8, dims * width // 8), shape(1, queries)],
-    )
-    gathered = lax.all_to_all(packed, "blk", 0, 0)
+    counts_vector = pltpu.VMEM((1, queries), jnp.int32)
+    packed, bounds, spread, target = call(
+        load_kernel,
+        [
+            pltpu.with_memory_space_constraint(array, pltpu.HBM)
+            for array in (samples, bounds, spread.reshape(1, dims), counts.reshape(1, queries))
+        ],
+        [
+            pltpu.VMEM((blocks, 8, dims * width // 8), jnp.float32),
+            pltpu.VMEM(bounds.shape, bounds.dtype),
+            pltpu.VMEM((1, dims), jnp.float32),
+            pltpu.VMEM((1, queries), jnp.float32),
+        ],
+        [pltpu.VMEM((dims, width), jnp.float32), counts_vector, pltpu.SemaphoreType.DMA((4,))],
+        placed=pl.ANY,
+    )
+    gathered = lax.all_to_all(
+        packed, "blk", 0, 0, axis_index_groups=[list(reversed(range(blocks)))]
+    )
     part = call(
         functools.partial(terms_kernel, width),
         [gathered, bounds, spread],
@@ -206,15 +234,13 @@
             pltpu.VMEM((total, 2 * queries), jnp.bfloat16),
         ],
     )
-    parts = everyone(part, "grp")
     log_est, share = call(
         functools.partial(finish_kernel, sample_total, query_total),
-        parts + [target],
+        everyone(part, "grp") + [target],
         [shape(1, queries), shape(blocks, 1, queries)],
     )
     shares = lax.all_to_all(share, "blk", 0, 0)
-    gradient = call(add_kernel, [shares], [shape(dims)])
-    return log_est.reshape(queries), gradient
+    return call(last_kernel, [shares, log_est], [shape(queries), shape(dims)])
 
 
 def solution(mesh):

time: 32.7 us -> 30.8 us (0.942)
  local copies, waits for them, and re-layouts: 2.13 us -> 0 us
  Pallas kernels: 2.68 us -> 3.05 us
    all_to_all x1, blocking collectives: 15.8 us -> 12.3 us  [on_device(): lax.all_to_all(packed, 'blk', 0, 0, axis_index_groups=[list(reversed(rang...]
    all_to_all x1, blocking collectives: 9.84 us -> 13.2 us  [on_device(): shares = lax.all_to_all(share, 'blk', 0, 0)]
    unnamed x10 -> x0, local copies, waits for them, and re-layouts: 2.13 us -> none
    pallas_call x4, Pallas kernels: 2.68 us -> 3.05 us  [call(): pl.pallas_call(kernel, out_shape=outs[0] if single else outs, in_specs=[p...]
where the time goes in v2:
time: 30.8 us; the launch traced here: 30.5 us
  blocking collectives  25.5 us (83%)
  Pallas kernels  3.05 us (10%)
  waiting for transfers between devices  1.18 us (4%)
  between operations  0.66 us (2%)
    all_to_all x1, blocking collectives, on_device(): shares = lax.all_to_all(share, 'blk', 0, 0)  13.2 us
    all_to_all x1, blocking collectives, on_device(): lax.all_to_all(packed, 'blk', 0, 0, axis_index_groups=[list(reversed(rang...  12.3 us
    pallas_call x4, Pallas kernels, call(): pl.pallas_call(kernel, out_shape=outs[0] if single else outs, in_specs=[p...  3.05 us
    ppermute x1, waiting for transfers between devices, everyone(): lax.ppermute(x, axis, [(i, i ^ offset) for i in range(size)])  1.18 us
  transfers between devices with their start and end apart: 1, of which 1 were waited for; matrix products, arithmetic and copies ran while one was open for 0% of the time, Pallas kernels for 0%

profile of v2, /device:TPU:0, one launch (start us, length us, event | category | flops | bytes accessed | tf_op | source)
XLA Modules:
  0.0 30.5 jit_solution(755177575988196721)
XLA Ops:
  0.6 0.8 %shard_map.59 = (f32[16,8,128]{2,1,0:T(8,128)S(1)}, s32[2,32,128]{2,1,0:T(8,128)S(1)}, f32[1,32]{1,0:T(1,128)S(1)}, f32[1,128]{1,0:T(1,128)S(1)}) custom-call(f32[32,32]{1,0:T(8,128)} %x_ref.1, s32[2,32,128]{2,1,0:T(8,128)} %bounds_ref.1, f32[1,32]{1,0:T(1,128)} %bitcast.2, s32[1,128]{1,0:T(1,128)} %bitcast.3), custom_call_target="tpu_custom_call" | custom-call | tf_op jit(solution)/shard_map/pallas_call | solution.py:185
  1.5 12.3 %all_to_all.10.blocks_ref = f32[16,8,128]{2,1,0:T(8,128)S(1)} all-to-all(f32[16,8,128]{2,1,0:T(8,128)S(1)} %get-tuple-element.8), channel_id=1, replica_groups={{30,28,26,24,22,20,18,16,14,12,10,8,6,4,2,0},{31,29,27,25,23,21,19,17,1..., dimensions={0} | all-to-all | bytes 131072 | tf_op jit(solution)/shard_map/all_to_all | solution.py:225
  13.8 1.6 %shard_map.60.refs_0_ = f32[40,128]{1,0:T(8,128)S(1)} custom-call(f32[16,8,128]{2,1,0:T(8,128)S(1)} %all_to_all.10.blocks_ref, s32[2,32,128]{2,1,0:T(8,128)S(1)} %get-tuple-element.9.bounds_ref, f32[1,32]{1,0:T(1,128)S(1)} %get-tuple-element.10.spread_ref), custom_call_target="tpu_custom_call" | custom-call | tf_op jit(solution)/shard_map/pallas_call | solution.py:185
  15.4 0.1 collective-permute-start
  15.5 1.2 %collective-permute-done.refs_1_ = f32[40,128]{1,0:T(8,128)S(1)} collective-permute-done((f32[40,128]{1,0:T(8,128)S(1)}, f32[40,128]{1,0:T(8,128)S(1)}, u32[]{:S(2)}, u32[]{:S(2)}) %collective-permute-start) | collective-permute-done | bytes 20512 | tf_op jit(solution)/shard_map/ppermute | solution.py:179
  16.6 0.1 shard_map.61
  16.8 13.2 %all_to_all.11.shares_ref = f32[16,1,128]{2,1,0:T(1,128)S(1)} all-to-all(f32[16,1,128]{2,1,0:T(1,128)S(1)} %get-tuple-element.12), channel_id=1, replica_groups=mesh['blk'=16,'grp'=2] {'blk'}, dimensions={0} | all-to-all | bytes 16384 | tf_op jit(solution)/shard_map/all_to_all | solution.py:242
  29.9 0.5 %shard_map.62 = (f32[128]{0:T(128)}, f32[32]{0:T(128)}) custom-call(f32[16,1,128]{2,1,0:T(1,128)S(1)} %all_to_all.11.shares_ref, f32[1,128]{1,0:T(1,128)S(1)} %get-tuple-element.13.held_log_ref), custom_call_target="tpu_custom_call" | custom-call | tf_op jit(solution)/shard_map/pallas_call | solution.py:185
Async XLA Ops:
  15.4 1.3 %collective-permute-start = (f32[40,128]{1,0:T(8,128)S(1)}, f32[40,128]{1,0:T(8,128)S(1)}, u32[]{:S(2)}, u32[]{:S(2)}) collective-permute-start(f32[40,128]{1,0:T(8,128)S(1)} %shard_map.60.refs_0_), channel_id=1, source_target_pairs={{0,1},{1,0},{2,3},{3,2},{4,5},{5,4},{6,7},{7,6},{8,9},{9,8},{10,11... | collective-permute-start | bytes 61448 | tf_op jit(solution)/shard_map/ppermute | solution.py:179
